TPU v7x, 256 devices: a whole 4x4x8 slice. The times are simulated.
256 devices in a mesh: slot: 16 (over z, core), hid: 16 (over y, x).
Axes of the slice: x: 4, y: 4, z: 8, core: 2. Of those that a mesh axis runs over, the one named last changes fastest.
Arguments:
- cotangent: bfloat16 [32768, 2048], P('slot', 'hid'), may hold values from -6 to 6
- hidden: bfloat16 [32768, 8192], P('slot', 'hid'), may hold values from -6 to 6
- weights: bfloat16 [16, 8192, 2048], P('slot', 'hid'), may hold values from -0.125 to 0.125
- slot_experts: int32 [16, 1], replicated, may hold values from 0 to 3
- next_experts: int32 [16, 1], replicated, may hold values from 0 to 3
- row_counts: int32 [16], replicated, may hold values from 1 to 2048, 20480 in all
- master: float32 [4, 8192, 2048], P(None, 'hid', 'slot'), may hold values from -3 to 3
- momentum: float32 [4, 8192, 2048], P(None, 'hid', 'slot'), may hold values from -96 to 96
Outputs:
- input_grad: bfloat16 [32768, 8192], P('slot', 'hid')
- new_momentum: float32 [4, 8192, 2048], P(None, 'hid', 'slot')
- new_master: float32 [4, 8192, 2048], P(None, 'hid', 'slot')
- placed: bfloat16 [16, 8192, 2048], P('slot', 'hid')
Inputs may be any that keep to these rules, and one draw needn't show every extreme that they name: `slot_experts`: every expert 0 to 3 is held by at least one slot. `next_experts`: every expert 0 to 3 is held by at least one slot. `row_counts`: the counts sum to 20480.
All inputs are finite; a program needn't handle non-finite values.
Results may differ from a plain program's by a relative error of at most 0.015.
Values may be sent and summed in bfloat16 or wider, within the bound.
No kernel may reach another device: no remote copies, remote signals or barrier semaphores. Data moves between devices by JAX's collectives and lax.ppermute only.
A program may use at most 128 MiB of HBM per device.

v0:
```python
import jax
import jax.numpy as jnp
from jax import lax
from jax.sharding import PartitionSpec as P

momentum_decay = 0.9
learn_rate = 0.01


def local(cotangent, hidden, weights, slot_experts, next_experts, row_counts, master, momentum):
    row_span = hidden.shape[0]
    own_slot = lax.axis_index("slot")
    live_count = lax.dynamic_index_in_dim(row_counts, own_slot, 0, keepdims=False)
    live_mask = (jnp.arange(row_span, dtype=jnp.int32) < live_count)[:, None].astype(
        cotangent.dtype
    )
    masked = cotangent * live_mask
    weight_rows = weights[0]
    shard_piece = lax.all_gather(masked, "hid", axis=1, tiled=True)
    hid_grad = lax.dot_general(
        shard_piece, weight_rows, (((1,), (1,)), ((), ())), preferred_element_type=jnp.float32
    )
    w_part = lax.dot_general(
        hidden, shard_piece, (((0,), (0,)), ((), ())), preferred_element_type=jnp.float32
    )
    w_grad = w_part
    hid_grad, w_grad = (hid_grad, w_grad)
    input_grad = hid_grad.astype(jnp.bfloat16)
    expert_count = master.shape[0]
    owners = (
        slot_experts[:, 0][None, :] == jnp.arange(expert_count, dtype=jnp.int32)[:, None]
    ).astype(jnp.float32)
    own_weight = lax.dynamic_index_in_dim(owners, own_slot, 1, keepdims=False)
    stacked = own_weight[:, None, None] * w_grad[None]
    expert_grad = lax.psum_scatter(
        stacked.astype(jnp.bfloat16), "slot", scatter_dimension=2, tiled=True
    ).astype(jnp.float32)
    new_momentum = momentum_decay * momentum + expert_grad
    new_master = master - learn_rate * new_momentum
    rounded = new_master.astype(jnp.bfloat16)
    gathered = lax.all_gather(rounded, "slot", axis=2, tiled=True)
    target = lax.dynamic_index_in_dim(next_experts[:, 0], own_slot, 0, keepdims=False)
    placed = lax.dynamic_index_in_dim(gathered, target, 0, keepdims=True)
    return (input_grad, new_momentum, new_master, placed)


def solution(mesh):
    return jax.shard_map(
        local,
        mesh=mesh,
        in_specs=(
            P("slot", "hid"),
            P("slot", "hid"),
            P("slot", "hid", None),
            P(),
            P(),
            P(),
            P(None, "hid", "slot"),
            P(None, "hid", "slot"),
        ),
        out_specs=(
            P("slot", "hid"),
            P(None, "hid", "slot"),
            P(None, "hid", "slot"),
            P("slot", "hid", None),
        ),
        check_vma=False,
    )
```

profile of v0, /device:TPU:1, one launch (start us, length us, event | category | flops | bytes accessed | tf_op | source)
XLA Modules:
  0.0 297.3 jit_solution(14528464055429409936)
XLA Ops:
  7.2 0.0 copy-start
  7.2 0.0 all-gather.3.cloned.1.call-start
  7.2 1.4 dynamic_slice.15
  8.6 0.6 fusion.1
  9.3 2.2 broadcast_multiply_fusion
  11.4 0.0 all-gather.3.cloned.1.call-update
  11.5 0.0 reduce-scatter.4.cloned.1.call-start
  11.5 1.2 dynamic-slice.1
  12.8 0.6 fusion.2
  13.4 84.5 %all-gather.3.cloned.1.call-done = bf16[2048,2048]{1,0:T(8,128)(2,1)} async-done(((bf16[2048,128]{1,0:T(8,128)(2,1)}), bf16[2048,2048]{1,0:T(8,128)(2,1)}) %all-gather.3.cloned.1.call-update) | async-done | bytes 8388624 | tf_op jit(solution)/shard_map/all_gather | solution.py:19
  97.9 0.0 copy-done
  97.9 9.8 %convolution_bitcast_fusion = f32[512,2048]{0,1:T(8,128)} fusion(bf16[2048,2048]{1,0:T(8,128)(2,1)} %all-gather.3.cloned.1.call-done, bf16[2048,512]{1,0:T(8,128)(2,1)S(1)} %copy-done), kind=kOutput, calls=%fused_computation.1 | convolution fusion | flops 4294967296 | bytes 14680064 | tf_op jit(solution)/shard_map/dot_general | solution.py:23
  107.7 5.5 %copy.13 = f32[512,2048]{1,0:T(8,128)} copy(f32[512,2048]{0,1:T(8,128)} %convolution_bitcast_fusion) | data formatting | bytes 8388608 | tf_op jit(solution)/shard_map/dot_general | solution.py:23
  113.1 8.0 %multiply_convert_fusion = bf16[4,512,2048]{2,1,0:T(8,128)(2,1)} fusion(f32[512,2048]{1,0:T(8,128)} %copy.13, f32[4]{0:T(128)S(1)} %fusion.2), kind=kLoop, calls=%fused_computation | loop fusion | flops 8388608 | bytes 12582928 | tf_op jit(solution)/shard_map/convert_element_type | solution.py:36
  121.1 14.6 %copy.14 = bf16[4,512,2048]{1,0,2:T(4,128)(2,1)} copy(bf16[4,512,2048]{2,1,0:T(8,128)(2,1)} %multiply_convert_fusion) | data formatting | bytes 16777216
  135.7 10.2 %copy.16 = bf16[256,8,4,512]{3,1,2,0:T(8,128)(2,1)} copy(bf16[256,8,4,512]{3,2,1,0:T(4,128)(2,1)} %bitcast.18) | data formatting | bytes 16777216
  146.0 0.0 reduce-scatter.4.cloned.1.call-update
  146.0 0.0 copy-start.1
  146.0 0.2 all-gather.5.cloned.1.call-start
  146.2 68.0 %reduce-scatter.4.cloned.1.call-done = bf16[128,2048]{1,0:T(8,128)(2,1)} async-done(((bf16[2048,2048]{1,0:T(8,128)(2,1)}), bf16[128,2048]{1,0:T(8,128)(2,1)}) %reduce-scatter.4.cloned.1.call-update) | async-done | bytes 524304
  214.3 1.4 reshape.21
  215.7 0.4 copy.15
  216.1 3.2 %fusion.3 = (bf16[4,512,128]{2,1,0:T(8,128)(2,1)}, f32[4,512,128]{2,1,0:T(8,128)}, f32[4,512,128]{2,1,0:T(8,128)}) fusion(f32[4,512,128]{2,1,0:T(8,128)} %param.14, bf16[4,512,128]{2,1,0:T(8,128)(2,1)S(1)} %copy.15, f32[4,512,128]{2,1,0:T(8,128)} %param.15), kind=kLoop, calls=%fused_computation.13 | loop fusion | flops 1572864 | bytes 5242880 | tf_op jit(solution)/shard_map/convert_element_type | solution.py:40
  219.4 0.0 all-gather.5.cloned.1.call-update
  219.4 0.0 copy-done.1
  219.4 0.6 constant_dynamic-slice_fusion
  221.9 9.9 %convolution_convert_fusion = bf16[2048,512]{1,0:T(8,128)(2,1)} fusion(bf16[2048,2048]{1,0:T(8,128)(2,1)} %all-gather.3.cloned.1.call-done, bf16[1,512,2048]{2,1,0:T(8,128)(2,1)} %param.10), kind=kOutput, calls=%fused_computation.2 | convolution fusion | flops 4296015872 | bytes 12582912 | tf_op jit(solution)/shard_map/dot_general | solution.py:20
  231.8 55.9 %all-gather.5.cloned.1.call-done = bf16[4,512,2048]{2,1,0:T(8,128)(2,1)} async-done(((bf16[4,512,128]{2,1,0:T(8,128)(2,1)}), bf16[4,512,2048]{2,1,0:T(8,128)(2,1)}) %all-gather.5.cloned.1.call-update) | async-done | bytes 8388624 | tf_op jit(solution)/shard_map/all_gather | solution.py:41
  287.6 3.2 %constant_dynamic-slice_fusion.1 = bf16[1,512,2048]{2,1,0:T(8,128)(2,1)} fusion(bf16[4,512,2048]{2,1,0:T(8,128)(2,1)} %all-gather.5.cloned.1.call-done, s32[]{:T(128)S(6)} %select_n.12), kind=kLoop, calls=%fused_computation.12 | loop fusion | bytes 4194308 | tf_op jit(solution)/shard_map/jit(dynamic_index_in_dim)/dynamic_slice | solution.py:43
Async XLA Ops:
  7.2 90.8 %copy-start = (bf16[2048,512]{1,0:T(8,128)(2,1)S(1)}, bf16[2048,512]{1,0:T(8,128)(2,1)}, u32[]{:S(2)}) copy-start(bf16[2048,512]{1,0:T(8,128)(2,1)} %param.9) | copy-start | bytes 6291460
  7.2 90.7 %all-gather.3.cloned.1.call-start = ((), (), s32[]{:S(2)}) async-start(), calls=%async_computation.1 | async-start | bytes 8912896 | tf_op jit(solution)/shard_map/all_gather | solution.py:19
  11.5 202.8 %reduce-scatter.4.cloned.1.call-start = ((), (), s32[]{:S(2)}) async-start(), calls=%async_computation.3 | async-start | bytes 8912896
  146.0 73.4 %copy-start.1 = (s32[16,1]{0,1:T(1,128)S(1)}, s32[16,1]{0,1:T(1,128)}, u32[]{:S(2)}) copy-start(s32[16,1]{0,1:T(1,128)} %param.12) | copy-start | bytes 196
  146.0 141.6 %all-gather.5.cloned.1.call-start = ((), (), s32[]{:S(2)}) async-start(), calls=%async_computation.2 | async-start | bytes 8912896 | tf_op jit(solution)/shard_map/all_gather | solution.py:41
Sparse Core Ops, SparseCore 0:
  11.6 86.2 all-gather.2
  146.1 68.1 reduce-scatter.3
  219.5 68.0 all-gather.4
where the time goes:
time: 298 us; the launch traced here: 297 us
  waiting for transfers between devices  208 us (70%)
  local copies, waits for them, and re-layouts  38.5 us (13%)
  matrix products  19.6 us (7%)
  between operations  15.7 us (5%)
  other arithmetic  14.7 us (5%)
    all_gather x1, waiting for transfers between devices, local(): shard_piece = lax.all_gather(masked, 'hid', axis=1, tiled=True)  84.5 us
    unnamed x4, waiting for transfers between devices  68.1 us
    all_gather x1, waiting for transfers between devices, local(): gathered = lax.all_gather(rounded, 'slot', axis=2, tiled=True)  55.9 us
    unnamed x8, local copies, waits for them, and re-layouts  26.7 us
    dot_general x1, matrix products, local(): lax.dot_general(shard_piece, weight_rows, (((1,), (1,)), ((), ())), prefe...  9.86 us
    dot_general x1, matrix products, local(): lax.dot_general(hidden, shard_piece, (((0,), (0,)), ((), ())), preferred_...  9.75 us
    convert_element_type x1, other arithmetic, local(): stacked.astype(jnp.bfloat16)  8 us
  transfers between devices with their start and end apart: 3, of which 3 were waited for; matrix products, arithmetic and copies ran while one was open for 4% of the time, Pallas kernels for 0%

commit v1 on v0

--- a/solution.py
+++ b/solution.py
@@ -5,6 +5,9 @@
 
 momentum_decay = 0.9
 learn_rate = 0.01
+_choose_ticks = lambda v0, shard_axis, in_dim: jnp.concatenate(
+    lax.all_to_all(jnp.stack(lax.axis_size(shard_axis) * [v0]), shard_axis, 0, 0), axis=in_dim
+)
 
 
 def local(cotangent, hidden, weights, slot_experts, next_experts, row_counts, master, momentum):
@@ -16,7 +19,7 @@
     )
     masked = cotangent * live_mask
     weight_rows = weights[0]
-    shard_piece = lax.all_gather(masked, "hid", axis=1, tiled=True)
+    shard_piece = _choose_ticks(masked, "hid", 1)
     hid_grad = lax.dot_general(
         shard_piece, weight_rows, (((1,), (1,)), ((), ())), preferred_element_type=jnp.float32
     )

time: 298 us -> 347 us (1.16)
  waiting for transfers between devices: 208 us -> 248 us
  starting transfers between devices: 0.3 us -> 8.03 us
  local copies, waits for them, and re-layouts: 38.5 us -> 42.4 us
    all_to_all x0 -> x1, waiting for transfers between devices: none -> 122 us  [lax.all_to_all(jnp.stack(lax.axis_size(shard_axis) * [v0]), shard_axis, 0...]
    all_gather x1 -> x0, waiting for transfers between devices: 84.5 us -> none  [local(): shard_piece = lax.all_gather(masked, 'hid', axis=1, tiled=True)]
    all_to_all x0 -> x1, starting transfers between devices: none -> 7.77 us  [lax.all_to_all(jnp.stack(lax.axis_size(shard_axis) * [v0]), shard_axis, 0...]
    another operation x0 -> x1, local copies, waits for them, and re-layouts: none -> 4.33 us  [jnp.stack(lax.axis_size(shard_axis) * [v0])]
    unnamed x4 -> x3, waiting for transfers between devices: 68.1 us -> 70.4 us
    unnamed x8 -> x16, local copies, waits for them, and re-layouts: 26.7 us -> 26.7 us
  transfers between devices with their start and end apart: 3 -> 3, of which waited for: 3 -> 3; matrix products, arithmetic and copies ran while one was open for 4% -> 3% of each run, Pallas kernels for 0% -> 0%
where the time goes in v1:
time: 347 us; the launch traced here: 346 us
  waiting for transfers between devices  248 us (71%)
  local copies, waits for them, and re-layouts  42.4 us (12%)
  matrix products  19.5 us (6%)
  between operations  16.1 us (5%)
  other arithmetic  12.4 us (4%)
  starting transfers between devices  8.03 us (2%)
    all_to_all x1, waiting for transfers between devices, lax.all_to_all(jnp.stack(lax.axis_size(shard_axis) * [v0]), shard_axis, 0...  122 us
    unnamed x3, waiting for transfers between devices  70.4 us
    all_gather x1, waiting for transfers between devices, local(): gathered = lax.all_gather(rounded, 'slot', axis=2, tiled=True)  55.7 us
    unnamed x16, local copies, waits for them, and re-layouts  26.7 us
    dot_general x1, matrix products, local(): lax.dot_general(shard_piece, weight_rows, (((1,), (1,)), ((), ())), prefe...  10 us
    dot_general x1, matrix products, local(): lax.dot_general(hidden, shard_piece, (((0,), (0,)), ((), ())), preferred_...  9.46 us
    convert_element_type x1, other arithmetic, local(): stacked.astype(jnp.bfloat16)  8.01 us
    all_to_all x1, starting transfers between devices, lax.all_to_all(jnp.stack(lax.axis_size(shard_axis) * [v0]), shard_axis, 0...  7.77 us
  transfers between devices with their start and end apart: 3, of which 3 were waited for; matrix products, arithmetic and copies ran while one was open for 3% of the time, Pallas kernels for 0%

profile of v1, /device:TPU:1, one launch (start us, length us, event | category | flops | bytes accessed | tf_op | source)
XLA Modules:
  0.0 346.4 jit_solution(2620301836180394556)
XLA Ops:
  7.2 0.0 copy-start
  7.2 1.4 dynamic_slice.15
  8.6 0.6 fusion.1
  9.2 1.4 broadcast_multiply_fusion
  10.6 0.2 copy.15
  10.8 4.3 %stack.2 = bf16[16,2048,128]{1,2,0:T(8,128)(2,1)} broadcast(bf16[2048,128]{0,1:T(8,128)(2,1)S(1)} %copy.15), dimensions={1,2} | broadcast | bytes 8912896 | tf_op jit(solution)/shard_map/stack | solution.py:9
  15.2 0.0 copy-start.4
  15.2 7.8 %all-to-all-start = ((bf16[16,2048,128]{1,2,0:T(8,128)(2,1)}), bf16[16,2048,128]{1,2,0:T(8,128)(2,1)}, u32[]{:S(2)}, u32[]{:S(2)}) async-start(bf16[16,2048,128]{1,2,0:T(8,128)(2,1)} %stack.2), calls=%async_computation | async-start | bytes 16777216 | tf_op jit(solution)/shard_map/all_to_all | solution.py:9
  22.9 0.0 reduce-scatter.4.cloned.1.call-start
  23.0 0.0 copy-done.4
  23.0 0.6 dynamic-slice.1
  23.6 0.6 fusion.2
  24.2 121.8 %all-to-all-done = bf16[16,2048,128]{1,2,0:T(8,128)(2,1)} async-done(((bf16[16,2048,128]{1,2,0:T(8,128)(2,1)}), bf16[16,2048,128]{1,2,0:T(8,128)(2,1)}, u32[]{:S(2)}, u32[]{:S(2)}) %all-to-all-start) | async-done | bytes 8388640 | tf_op jit(solution)/shard_map/all_to_all | solution.py:9
  146.1 0.0 copy-done
  146.1 9.5 %convolution_bitcast_fusion = f32[512,2048]{0,1:T(8,128)} fusion(bf16[2048,2048]{0,1:T(8,128)(2,1)} %bitcast.2, bf16[2048,512]{1,0:T(8,128)(2,1)S(1)} %copy-done), kind=kOutput, calls=%fused_computation.1 | convolution fusion | flops 4294967296 | bytes 14680064 | tf_op jit(solution)/shard_map/dot_general | solution.py:26
  155.5 5.4 %copy.16 = f32[512,2048]{1,0:T(8,128)} copy(f32[512,2048]{0,1:T(8,128)} %convolution_bitcast_fusion) | data formatting | bytes 8388608 | tf_op jit(solution)/shard_map/dot_general | solution.py:26
  161.0 8.0 %multiply_convert_fusion = bf16[4,512,2048]{2,1,0:T(8,128)(2,1)} fusion(f32[512,2048]{1,0:T(8,128)} %copy.16, f32[4]{0:T(128)S(1)} %fusion.2), kind=kLoop, calls=%fused_computation | loop fusion | flops 8388608 | bytes 12582928 | tf_op jit(solution)/shard_map/convert_element_type | solution.py:39
  169.0 14.6 %copy.17 = bf16[4,512,2048]{1,0,2:T(4,128)(2,1)} copy(bf16[4,512,2048]{2,1,0:T(8,128)(2,1)} %multiply_convert_fusion) | data formatting | bytes 16777216
  183.6 10.2 %copy.19 = bf16[256,8,4,512]{3,1,2,0:T(8,128)(2,1)} copy(bf16[256,8,4,512]{3,2,1,0:T(4,128)(2,1)} %bitcast.21) | data formatting | bytes 16777216
  193.8 0.0 copy-start.2
  193.8 0.0 copy-start.3
  193.8 0.0 copy-start.5
  193.8 0.0 reduce-scatter.4.cloned.1.call-update
  193.8 0.2 all-gather.2.cloned.1.call-start
  194.1 70.4 %reduce-scatter.4.cloned.1.call-done = bf16[128,2048]{1,0:T(8,128)(2,1)} async-done(((bf16[2048,2048]{1,0:T(8,128)(2,1)}), bf16[128,2048]{1,0:T(8,128)(2,1)}) %reduce-scatter.4.cloned.1.call-update) | async-done | bytes 524304
  264.5 1.4 reshape.31
  265.9 0.4 copy.18
  266.3 0.0 copy-done.2
  266.3 0.0 copy-done.3
  266.3 1.7 fusion.3
  268.0 0.0 all-gather.2.cloned.1.call-update
  268.1 0.0 copy-done.5
  268.1 0.6 constant_dynamic-slice_fusion
  270.6 0.0 copy-start.1
  270.6 10.0 %convolution_convert_fusion = bf16[2048,512]{1,0:T(8,128)(2,1)} fusion(bf16[2048,2048]{0,1:T(8,128)(2,1)} %bitcast.2, bf16[1,512,2048]{2,1,0:T(8,128)(2,1)} %param.10), kind=kOutput, calls=%fused_computation.2 | convolution fusion | flops 4296015872 | bytes 12582912 | tf_op jit(solution)/shard_map/dot_general | solution.py:23
  280.6 55.7 %all-gather.2.cloned.1.call-done = bf16[4,512,2048]{2,1,0:T(8,128)(2,1)} async-done(((bf16[4,512,128]{2,1,0:T(8,128)(2,1)}), bf16[4,512,2048]{2,1,0:T(8,128)(2,1)}) %all-gather.2.cloned.1.call-update) | async-done | bytes 8388624 | tf_op jit(solution)/shard_map/all_gather | solution.py:44
  336.4 3.2 constant_dynamic-slice_fusion.1
  339.5 0.0 copy-done.1
Async XLA Ops:
  7.2 138.9 %copy-start = (bf16[2048,512]{1,0:T(8,128)(2,1)S(1)}, bf16[2048,512]{1,0:T(8,128)(2,1)}, u32[]{:S(2)}) copy-start(bf16[2048,512]{1,0:T(8,128)(2,1)} %param.9) | copy-start | bytes 6291460
  15.2 7.8 %copy-start.4 = (s32[16,1]{0,1:T(1,128)S(1)}, s32[16,1]{0,1:T(1,128)}, u32[]{:S(2)}) copy-start(s32[16,1]{0,1:T(1,128)} %param.11) | copy-start | bytes 196
  15.2 130.9 %all-to-all-start = ((bf16[16,2048,128]{1,2,0:T(8,128)(2,1)}), bf16[16,2048,128]{1,2,0:T(8,128)(2,1)}, u32[]{:S(2)}, u32[]{:S(2)}) async-start(bf16[16,2048,128]{1,2,0:T(8,128)(2,1)} %stack.2), calls=%async_computation | async-start | bytes 16777216 | tf_op jit(solution)/shard_map/all_to_all | solution.py:9
  22.9 241.5 %reduce-scatter.4.cloned.1.call-start = ((), (), s32[]{:S(2)}) async-start(), calls=%async_computation.3 | async-start | bytes 8912896
  193.8 72.5 %copy-start.2 = (f32[4,512,128]{2,1,0:T(8,128)S(1)}, f32[4,512,128]{2,1,0:T(8,128)}, u32[]{:S(2)}) copy-start(f32[4,512,128]{2,1,0:T(8,128)} %param.14) | copy-start | bytes 3145732
  193.8 72.5 %copy-start.3 = (f32[4,512,128]{2,1,0:T(8,128)S(1)}, f32[4,512,128]{2,1,0:T(8,128)}, u32[]{:S(2)}) copy-start(f32[4,512,128]{2,1,0:T(8,128)} %param.15) | copy-start | bytes 3145732
  193.8 74.3 %copy-start.5 = (s32[16,1]{0,1:T(1,128)S(1)}, s32[16,1]{0,1:T(1,128)}, u32[]{:S(2)}) copy-start(s32[16,1]{0,1:T(1,128)} %param.12) | copy-start | bytes 196
  193.8 142.6 %all-gather.2.cloned.1.call-start = ((), (), s32[]{:S(2)}) async-start(), calls=%async_computation.2 | async-start | bytes 8912896 | tf_op jit(solution)/shard_map/all_gather | solution.py:44
  270.6 69.0 %copy-start.1 = (bf16[2048,512]{1,0:T(8,128)(2,1)S(1)}, bf16[2048,512]{1,0:T(8,128)(2,1)}, u32[]{:S(2)}) copy-start(bf16[2048,512]{1,0:T(8,128)(2,1)} %param.9) | copy-start | bytes 6291460
Sparse Core Ops, SparseCore 0:
  193.9 70.4 reduce-scatter.3
  268.2 68.1 all-gather.1
